TPU v7x, 32 devices: a whole 2x2x4 slice. The times are simulated.
32 devices in a mesh: segment: 4 (over x, core), seq: 8 (over z, y).
Axes of the slice: x: 2, y: 2, z: 4, core: 2. Of those that a mesh axis runs over, the one named last changes fastest.
Arguments:
- latent: bfloat16 [3072, 1536], P('seq'), may hold values from -4 to 4
- stale_kv: bfloat16 [4, 2, 3072, 1536], P('segment', None, 'seq'), may hold values from -3 to 3
- query_weight: bfloat16 [4, 1536, 1536], P('segment', 'seq'), may hold values from -0.15625 to 0.15625
- key_weight: bfloat16 [4, 1536, 1536], P('segment', 'seq'), may hold values from -0.15625 to 0.15625
- value_weight: bfloat16 [4, 1536, 1536], P('segment', 'seq'), may hold values from -0.15625 to 0.15625
- out_weight: bfloat16 [4, 1536, 1536], P('segment', 'seq'), may hold values from -0.3125 to 0.3125
- query_gain: float32 [4, 128], P('segment'), may hold values from 0.5 to 2
- key_gain: float32 [4, 128], P('segment'), may hold values from 0.5 to 2
- tile_mask: int32 [48, 6], P('seq'), may hold values from -1 to 47, as said below
Outputs:
- section_out: bfloat16 [4, 3072, 1536], P('segment', 'seq')
Inputs may be any that keep to these rules, and one draw needn't show every extreme that they name: `tile_mask`: row g lists the key tiles of query tile g: slot 0 holds g itself, the next slots distinct other tiles whose tile-frame (tile number // 6) differs from that of g by at most one, and the remaining slots -1. Every row lists two or more tiles, and some row lists 6.
All inputs are finite; a program needn't handle non-finite values.
Results may differ from a plain program's by a relative error of at most 0.027.
Values may be sent and summed in bfloat16 or wider, within the bound.
A program may use at most 128 MiB of HBM per device.

v0:
```python
import math

import jax
import jax.numpy as jnp
from jax import lax
from jax.sharding import PartitionSpec as P

D = 1536
HEADS = 12
HEAD = 128
TILE = 64
PATCHES = 3
TPP = 2


epsilon = 1e-06


def extended(cells, sides, width):
    for axis, dim in sides:
        count = lax.axis_size(axis)
        ends = count - 1
        head = lax.slice_in_dim(cells, 0, width, axis=dim)
        tail = lax.slice_in_dim(cells, cells.shape[dim] - width, cells.shape[dim], axis=dim)
        cells = jnp.concatenate(
            [
                lax.ppermute(tail, axis, [(i, (i + 1) % count) for i in range(ends)]),
                cells,
                lax.ppermute(head, axis, [((i + 1) % count, i) for i in range(ends)]),
            ],
            axis=dim,
        )
    return cells


def from_behind(value, axis, by):
    count = lax.axis_size(axis)
    pairs = [(i, i + by) for i in range(count) if 0 <= i + by < count]
    return lax.ppermute(value, axis, pairs)


def head_normed(projected, gain):
    n_rows = projected.shape[0]
    heads = projected.reshape(n_rows, HEADS, HEAD)
    scaled = heads * lax.rsqrt(jnp.mean(heads * heads, axis=-1, keepdims=True) + epsilon)
    return (scaled * gain).reshape(n_rows, D).astype(jnp.bfloat16)


def keys_values(inputs, weight_k, weight_v, gain_k):
    keys = head_normed(jnp.dot(inputs, weight_k, preferred_element_type=jnp.float32), gain_k)
    values = jnp.dot(inputs, weight_v, preferred_element_type=jnp.float32).astype(jnp.bfloat16)
    return jnp.stack([keys, values])


def attend(queries, blocks, tile_index, usable):
    n_query = tile_index.shape[0]
    key_heads = jnp.take(blocks[0], tile_index, axis=0).reshape(n_query, -1, HEADS, HEAD)
    value_heads = jnp.take(blocks[1], tile_index, axis=0).reshape(n_query, -1, HEADS, HEAD)
    query_heads = queries.reshape(n_query, -1, HEADS, HEAD)
    scores = jnp.einsum(
        "pthe,pkhe->phtk", query_heads, key_heads, preferred_element_type=jnp.float32
    ) / math.sqrt(HEAD)
    listed = jnp.repeat(usable, TILE, axis=1).astype(jnp.float32)
    weights = jnp.exp(scores) * listed[:, None, None, :]
    totals = jnp.sum(weights, axis=-1)
    summed = jnp.einsum(
        "phtk,pkhe->pthe",
        weights.astype(jnp.bfloat16),
        value_heads,
        preferred_element_type=jnp.float32,
    )
    return summed / jnp.swapaxes(totals, 1, 2)[..., None]


def per_device(
    latent,
    stale_kv,
    query_weight,
    key_weight,
    value_weight,
    out_weight,
    query_gain,
    key_gain,
    tile_mask,
):
    tok_dev = latent.shape[0]
    patch_rows = tok_dev // PATCHES
    tiles_dev = tile_mask.shape[0]
    segment_id = lax.axis_index("segment")
    frame_id = lax.axis_index("seq")
    rounds = PATCHES + lax.axis_size("segment") - 1
    full_q, full_k, full_v, full_out = (
        lax.all_gather(query_weight[0], "seq", axis=0, tiled=True),
        lax.all_gather(key_weight[0], "seq", axis=0, tiled=True),
        lax.all_gather(value_weight[0], "seq", axis=0, tiled=True),
        lax.all_gather(out_weight[0], "seq", axis=0, tiled=True),
    )
    gain_q = query_gain[0]
    gain_k = key_gain[0]
    local_kv = stale_kv[0]
    window = extended(local_kv, (("seq", 1),), tok_dev)
    zero_rows = jnp.zeros((patch_rows, D), jnp.bfloat16)
    zero_pair = jnp.zeros((2, patch_rows, D), jnp.bfloat16)

    def project(inputs):
        fresh_q = head_normed(jnp.dot(inputs, full_q, preferred_element_type=jnp.float32), gain_q)
        return (fresh_q, keys_values(inputs, full_k, full_v, gain_k))

    def skip_project(inputs):
        return (zero_rows, zero_pair)

    def advance(round_id, carry):
        window, received, result = carry
        patch_id = round_id - segment_id
        active = (patch_id >= 0) & (patch_id < PATCHES)
        current = jnp.clip(patch_id, 0, PATCHES - 1)
        offset = current * patch_rows
        entering = lax.dynamic_slice_in_dim(latent, offset, patch_rows, 0)
        inputs = jnp.where(segment_id == 0, entering, received)
        fresh_q, own_kv = lax.cond(active, project, skip_project, inputs)
        spread = extended(own_kv, (("seq", 1),), patch_rows)
        trailing = spread[:, :patch_rows]
        leading = spread[:, 2 * patch_rows :]

        def finish(state):
            former, stored = state
            updated = lax.dynamic_update_slice_in_dim(former, trailing, offset, 1)
            updated = lax.dynamic_update_slice_in_dim(updated, own_kv, tok_dev + offset, 1)
            updated = lax.dynamic_update_slice_in_dim(updated, leading, 2 * tok_dev + offset, 1)
            listing = lax.dynamic_slice_in_dim(tile_mask, current * TPP, TPP, 0)
            usable = listing >= 0
            tile_index = jnp.where(usable, listing - (frame_id - 1) * tiles_dev, 0)
            blocks = updated.reshape(2, 3 * tiles_dev, TILE, D)
            attention = attend(fresh_q.reshape(TPP, TILE, D), blocks, tile_index, usable)
            attention_b = attention.reshape(patch_rows, D).astype(jnp.bfloat16)
            mixed = jnp.dot(attention_b, full_out, preferred_element_type=jnp.float32)
            leaving = (inputs.astype(jnp.float32) + mixed).astype(jnp.bfloat16)
            stored = lax.dynamic_update_slice_in_dim(stored, leaving, offset, 0)
            return (updated, stored, leaving)

        def remain(state):
            return (state[0], state[1], zero_rows)

        window, result, leaving = lax.cond(active, finish, remain, (window, result))
        received = from_behind(leaving, "segment", 1)
        return (window, received, result)

    initial = (window, zero_rows, jnp.zeros((tok_dev, D), jnp.bfloat16))
    final_state = lax.fori_loop(0, rounds, advance, initial)
    return final_state[2][None]


def solution(mesh):
    return jax.shard_map(
        per_device,
        mesh=mesh,
        in_specs=(
            P("seq", None),
            P("segment", None, "seq", None),
            P("segment", "seq", None),
            P("segment", "seq", None),
            P("segment", "seq", None),
            P("segment", "seq", None),
            P("segment", None),
            P("segment", None),
            P("seq", None),
        ),
        out_specs=P("segment", "seq", None),
        check_vma=False,
    )
```

profile of v0, /device:TPU:19, one launch (start us, length us, event | category | flops | bytes accessed | tf_op | source)
XLA Modules:
  0.0 1032.9 jit_solution(3498116346240532675)
XLA Ops:
  15.5 124.8 %collective-permute-done.3 = bf16[2,384,1536]{2,1,0:T(8,128)(2,1)} collective-permute-done((bf16[2,384,1536]{2,1,0:T(8,128)(2,1)S(1)}, bf16[2,384,1536]{2,1,0:T(8,128)(2,1)}, u32[]{:S(2)}, u32[]{:S(2)}) %collective-permute-start.3) | collective-permute-done | bytes 2359328 | tf_op jit(solution)/shard_map/ppermute | solution.py:27
  144.3 5.7 pad_maximum_fusion.1
  150.0 13.2 %all-gather.9.cloned.1.call-done = bf16[1,1536,1536]{2,1,0:T(8,128)(2,1)} async-done(((bf16[1,192,1536]{2,1,0:T(8,128)(2,1)}), bf16[1,1536,1536]{2,1,0:T(8,128)(2,1)}) %all-gather.9.cloned.1.call-update) | async-done | bytes 4718608 | tf_op jit(solution)/shard_map/all_gather | solution.py:93
  163.2 80.0 %all-gather.11.cloned.1.call-done = bf16[1,1536,1536]{2,1,0:T(8,128)(2,1)} async-done(((bf16[1,192,1536]{2,1,0:T(8,128)(2,1)}), bf16[1,1536,1536]{2,1,0:T(8,128)(2,1)}) %all-gather.11.cloned.1.call-update) | async-done | bytes 4718608 | tf_op jit(solution)/shard_map/all_gather | solution.py:94
  243.2 80.2 %all-gather.13.cloned.1.call-done = bf16[1,1536,1536]{2,1,0:T(8,128)(2,1)} async-done(((bf16[1,192,1536]{2,1,0:T(8,128)(2,1)}), bf16[1,1536,1536]{2,1,0:T(8,128)(2,1)}) %all-gather.13.cloned.1.call-update) | async-done | bytes 4718608 | tf_op jit(solution)/shard_map/all_gather | solution.py:95
  323.5 80.1 %all-gather.15.cloned.1.call-done = bf16[1,1536,1536]{2,1,0:T(8,128)(2,1)} async-done(((bf16[1,192,1536]{2,1,0:T(8,128)(2,1)}), bf16[1,1536,1536]{2,1,0:T(8,128)(2,1)}) %all-gather.15.cloned.1.call-update) | async-done | bytes 4718608 | tf_op jit(solution)/shard_map/all_gather | solution.py:96
  404.7 621.7 %while.18 = (s32[]{:T(128)}, bf16[2,1152,1536]{2,1,0:T(8,128)(2,1)}, bf16[128,1536]{1,0:T(8,128)(2,1)S(1)}, bf16[384,1536]{1,0:T(8,128)(2,1)}, s32[]{:T(128)}, /...) while((s32[]{:T(128)}, ...), condition=%wide.region_8.10_spmd, body=%wide.region_0.9_spmd.sunk | while | flops 2727545344 | bytes 147957200 | solution.py:149
  412.1 28.6 %collective-permute-done = bf16[2,128,1536]{2,1,0:T(8,128)(2,1)S(1)} collective-permute-done((bf16[2,128,1536]{2,1,0:T(8,128)(2,1)S(1)}, bf16[2,128,1536]{2,1,0:T(8,128)(2,1)S(1)}, u32[]{:S(2)}, u32[]{:S(2)}) %collective-permute-start) | collective-permute-done | bytes 786464 | tf_op jit(solution)/shard_map/while/body/eval_jaxpr/ppermute | solution.py:27
  457.1 24.9 %collective-permute-done = bf16[2,128,1536]{2,1,0:T(8,128)(2,1)S(1)} collective-permute-done((bf16[2,128,1536]{2,1,0:T(8,128)(2,1)S(1)}, bf16[2,128,1536]{2,1,0:T(8,128)(2,1)S(1)}, u32[]{:S(2)}, u32[]{:S(2)}) %collective-permute-start) | collective-permute-done | bytes 786464 | tf_op jit(solution)/shard_map/while/body/eval_jaxpr/ppermute | solution.py:27
  482.0 8.0 collective-permute-done.1
  502.0 13.1 %collective-permute-done = bf16[2,128,1536]{2,1,0:T(8,128)(2,1)S(1)} collective-permute-done((bf16[2,128,1536]{2,1,0:T(8,128)(2,1)S(1)}, bf16[2,128,1536]{2,1,0:T(8,128)(2,1)S(1)}, u32[]{:S(2)}, u32[]{:S(2)}) %collective-permute-start) | collective-permute-done | bytes 786464 | tf_op jit(solution)/shard_map/while/body/eval_jaxpr/ppermute | solution.py:27
  519.9 186.1 %collective-permute-done.2 = bf16[128,1536]{1,0:T(8,128)(2,1)S(1)} collective-permute-done((bf16[128,1536]{1,0:T(8,128)(2,1)}, bf16[128,1536]{1,0:T(8,128)(2,1)S(1)}, u32[]{:S(2)}, u32[]{:S(2)}) %collective-permute-start.2) | collective-permute-done | bytes 393248 | tf_op jit(solution)/shard_map/while/body/eval_jaxpr/ppermute | solution.py:39
  707.1 9.9 conditional.4
  723.2 13.1 %collective-permute-done = bf16[2,128,1536]{2,1,0:T(8,128)(2,1)S(1)} collective-permute-done((bf16[2,128,1536]{2,1,0:T(8,128)(2,1)S(1)}, bf16[2,128,1536]{2,1,0:T(8,128)(2,1)S(1)}, u32[]{:S(2)}, u32[]{:S(2)}) %collective-permute-start) | collective-permute-done | bytes 786464 | tf_op jit(solution)/shard_map/while/body/eval_jaxpr/ppermute | solution.py:27
  739.0 53.9 %conditional.5 = (bf16[2,1152,1536]{2,1,0:T(8,128)(2,1)}, bf16[384,1536]{1,0:T(8,128)(2,1)}, bf16[128,1536]{1,0:T(8,128)(2,1)}) conditional(s32[]{:T(128)} %convert_element_type.58, (bf16[2,1152,1536]{2,1,0:T(8,128)(2,1)}, bf16[384,1536]{1,0:T(8,128)(2,1)}) %tuple.60, (s32[]{:T(128)}, bf16[2,1152,1536]{2,1,0:T(8,128)(2,1)}, ...), branch_computations={%region_5.5_spmd, %region_6.8_spmd} | conditional | flops 912850560 | bytes 86146920 | solution.py:144
  770.5 5.5 reshape.55
  794.3 20.1 %collective-permute-done.2 = bf16[128,1536]{1,0:T(8,128)(2,1)S(1)} collective-permute-done((bf16[128,1536]{1,0:T(8,128)(2,1)}, bf16[128,1536]{1,0:T(8,128)(2,1)S(1)}, u32[]{:S(2)}, u32[]{:S(2)}) %collective-permute-start.2) | collective-permute-done | bytes 393248 | tf_op jit(solution)/shard_map/while/body/eval_jaxpr/ppermute | solution.py:39
  815.5 9.9 conditional.4
  831.6 24.9 %collective-permute-done = bf16[2,128,1536]{2,1,0:T(8,128)(2,1)S(1)} collective-permute-done((bf16[2,128,1536]{2,1,0:T(8,128)(2,1)S(1)}, bf16[2,128,1536]{2,1,0:T(8,128)(2,1)S(1)}, u32[]{:S(2)}, u32[]{:S(2)}) %collective-permute-start) | collective-permute-done | bytes 786464 | tf_op jit(solution)/shard_map/while/body/eval_jaxpr/ppermute | solution.py:27
  856.5 8.0 collective-permute-done.1
  864.5 53.9 %conditional.5 = (bf16[2,1152,1536]{2,1,0:T(8,128)(2,1)}, bf16[384,1536]{1,0:T(8,128)(2,1)}, bf16[128,1536]{1,0:T(8,128)(2,1)}) conditional(s32[]{:T(128)} %convert_element_type.58, (bf16[2,1152,1536]{2,1,0:T(8,128)(2,1)}, bf16[384,1536]{1,0:T(8,128)(2,1)}) %tuple.60, (s32[]{:T(128)}, bf16[2,1152,1536]{2,1,0:T(8,128)(2,1)}, ...), branch_computations={%region_5.5_spmd, %region_6.8_spmd} | conditional | flops 912850560 | bytes 86146920 | solution.py:144
  923.3 9.9 conditional.4
  939.4 26.1 %collective-permute-done = bf16[2,128,1536]{2,1,0:T(8,128)(2,1)S(1)} collective-permute-done((bf16[2,128,1536]{2,1,0:T(8,128)(2,1)S(1)}, bf16[2,128,1536]{2,1,0:T(8,128)(2,1)S(1)}, u32[]{:S(2)}, u32[]{:S(2)}) %collective-permute-start) | collective-permute-done | bytes 786464 | tf_op jit(solution)/shard_map/while/body/eval_jaxpr/ppermute | solution.py:27
  968.8 53.8 %conditional.5 = (bf16[2,1152,1536]{2,1,0:T(8,128)(2,1)}, bf16[384,1536]{1,0:T(8,128)(2,1)}, bf16[128,1536]{1,0:T(8,128)(2,1)}) conditional(s32[]{:T(128)} %convert_element_type.58, (bf16[2,1152,1536]{2,1,0:T(8,128)(2,1)}, bf16[384,1536]{1,0:T(8,128)(2,1)}) %tuple.60, (s32[]{:T(128)}, bf16[2,1152,1536]{2,1,0:T(8,128)(2,1)}, ...), branch_computations={%region_5.5_spmd, %region_6.8_spmd} | conditional | flops 912850560 | bytes 86146920 | solution.py:144
  (222 shorter events, 279.1 us)
Async XLA Ops:
  6.5 156.7 %all-gather.9.cloned.1.call-start = ((), (), s32[]{:S(2)}) async-start(), calls=%async_computation | async-start | bytes 5308416 | tf_op jit(solution)/shard_map/all_gather | solution.py:93
  7.3 236.0 %all-gather.11.cloned.1.call-start = ((), (), s32[]{:S(2)}) async-start(), calls=%async_computation.1 | async-start | bytes 5308416 | tf_op jit(solution)/shard_map/all_gather | solution.py:94
  8.0 315.5 %all-gather.13.cloned.1.call-start = ((), (), s32[]{:S(2)}) async-start(), calls=%async_computation.2 | async-start | bytes 5308416 | tf_op jit(solution)/shard_map/all_gather | solution.py:95
  8.7 394.8 %all-gather.15.cloned.1.call-start = ((), (), s32[]{:S(2)}) async-start(), calls=%async_computation.3 | async-start | bytes 5308416 | tf_op jit(solution)/shard_map/all_gather | solution.py:96
  9.3 131.0 %collective-permute-start.3 = (bf16[2,384,1536]{2,1,0:T(8,128)(2,1)S(1)}, bf16[2,384,1536]{2,1,0:T(8,128)(2,1)}, u32[]{:S(2)}, u32[]{:S(2)}) collective-permute-start(bf16[2,384,1536]{2,1,0:T(8,128)(2,1)S(1)} %bitcast.66), channel_id=1, source_target_pairs={{0,1},{1,2},{2,3},{3,4},{4,5},{5,6},{6,7},{8,9},{9,10},{10,11},{11... | collective-permute-start | bytes 7077896 | tf_op jit(solution)/shard_map/ppermute | solution.py:27
  12.5 131.8 %collective-permute-start.4 = (bf16[2,384,1536]{2,1,0:T(8,128)(2,1)S(1)}, bf16[2,384,1536]{2,1,0:T(8,128)(2,1)}, u32[]{:S(2)}, u32[]{:S(2)}) collective-permute-start(bf16[2,384,1536]{2,1,0:T(8,128)(2,1)S(1)} %bitcast.67), channel_id=1, source_target_pairs={{1,0},{2,1},{3,2},{4,3},{5,4},{6,5},{7,6},{9,8},{10,9},{11,10},{12... | collective-permute-start | bytes 7077896 | tf_op jit(solution)/shard_map/ppermute | solution.py:29
  405.9 34.8 %collective-permute-start = (bf16[2,128,1536]{2,1,0:T(8,128)(2,1)S(1)}, bf16[2,128,1536]{2,1,0:T(8,128)(2,1)S(1)}, u32[]{:S(2)}, u32[]{:S(2)}) collective-permute-start(bf16[2,128,1536]{2,1,0:T(8,128)(2,1)S(1)} %get-tuple-element.507), channel_id=1, source_target_pairs={{0,1},{1,2},{2,3},{3,4},{4,5},{5,6},{6,7},{8,9},{9,10},{10,11},{11... | collective-permute-start | bytes 2359304 | tf_op jit(solution)/shard_map/while/body/eval_jaxpr/ppermute | solution.py:27
  408.1 36.9 %collective-permute-start.1 = (bf16[2,128,1536]{2,1,0:T(8,128)(2,1)S(1)}, bf16[2,128,1536]{2,1,0:T(8,128)(2,1)S(1)}, u32[]{:S(2)}, u32[]{:S(2)}) collective-permute-start(bf16[2,128,1536]{2,1,0:T(8,128)(2,1)S(1)} %get-tuple-element.507), channel_id=1, source_target_pairs={{1,0},{2,1},{3,2},{4,3},{5,4},{6,5},{7,6},{9,8},{10,9},{11,10},{12... | collective-permute-start | bytes 2359304 | tf_op jit(solution)/shard_map/while/body/eval_jaxpr/ppermute | solution.py:29
  445.8 3.8 collective-permute-start.2
  450.9 31.1 %collective-permute-start = (bf16[2,128,1536]{2,1,0:T(8,128)(2,1)S(1)}, bf16[2,128,1536]{2,1,0:T(8,128)(2,1)S(1)}, u32[]{:S(2)}, u32[]{:S(2)}) collective-permute-start(bf16[2,128,1536]{2,1,0:T(8,128)(2,1)S(1)} %get-tuple-element.507), channel_id=1, source_target_pairs={{0,1},{1,2},{2,3},{3,4},{4,5},{5,6},{6,7},{8,9},{9,10},{10,11},{11... | collective-permute-start | bytes 2359304 | tf_op jit(solution)/shard_map/while/body/eval_jaxpr/ppermute | solution.py:27
  452.8 37.2 %collective-permute-start.1 = (bf16[2,128,1536]{2,1,0:T(8,128)(2,1)S(1)}, bf16[2,128,1536]{2,1,0:T(8,128)(2,1)S(1)}, u32[]{:S(2)}, u32[]{:S(2)}) collective-permute-start(bf16[2,128,1536]{2,1,0:T(8,128)(2,1)S(1)} %get-tuple-element.507), channel_id=1, source_target_pairs={{1,0},{2,1},{3,2},{4,3},{5,4},{6,5},{7,6},{9,8},{10,9},{11,10},{12... | collective-permute-start | bytes 2359304 | tf_op jit(solution)/shard_map/while/body/eval_jaxpr/ppermute | solution.py:29
  490.8 3.8 collective-permute-start.2
  495.8 19.3 %collective-permute-start = (bf16[2,128,1536]{2,1,0:T(8,128)(2,1)S(1)}, bf16[2,128,1536]{2,1,0:T(8,128)(2,1)S(1)}, u32[]{:S(2)}, u32[]{:S(2)}) collective-permute-start(bf16[2,128,1536]{2,1,0:T(8,128)(2,1)S(1)} %get-tuple-element.507), channel_id=1, source_target_pairs={{0,1},{1,2},{2,3},{3,4},{4,5},{5,6},{6,7},{8,9},{9,10},{10,11},{11... | collective-permute-start | bytes 2359304 | tf_op jit(solution)/shard_map/while/body/eval_jaxpr/ppermute | solution.py:27
  497.7 20.1 %collective-permute-start.1 = (bf16[2,128,1536]{2,1,0:T(8,128)(2,1)S(1)}, bf16[2,128,1536]{2,1,0:T(8,128)(2,1)S(1)}, u32[]{:S(2)}, u32[]{:S(2)}) collective-permute-start(bf16[2,128,1536]{2,1,0:T(8,128)(2,1)S(1)} %get-tuple-element.507), channel_id=1, source_target_pairs={{1,0},{2,1},{3,2},{4,3},{5,4},{6,5},{7,6},{9,8},{10,9},{11,10},{12... | collective-permute-start | bytes 2359304 | tf_op jit(solution)/shard_map/while/body/eval_jaxpr/ppermute | solution.py:29
  518.6 187.3 %collective-permute-start.2 = (bf16[128,1536]{1,0:T(8,128)(2,1)}, bf16[128,1536]{1,0:T(8,128)(2,1)S(1)}, u32[]{:S(2)}, u32[]{:S(2)}) collective-permute-start(bf16[128,1536]{1,0:T(8,128)(2,1)} %get-tuple-element.510), channel_id=1, source_target_pairs={{0,8},{8,16},{16,24},{1,9},{9,17},{17,25},{2,10},{10,18},{18,26},{... | collective-permute-start | bytes 1179656 | tf_op jit(solution)/shard_map/while/body/eval_jaxpr/ppermute | solution.py:39
  717.0 19.3 %collective-permute-start = (bf16[2,128,1536]{2,1,0:T(8,128)(2,1)S(1)}, bf16[2,128,1536]{2,1,0:T(8,128)(2,1)S(1)}, u32[]{:S(2)}, u32[]{:S(2)}) collective-permute-start(bf16[2,128,1536]{2,1,0:T(8,128)(2,1)S(1)} %get-tuple-element.507), channel_id=1, source_target_pairs={{0,1},{1,2},{2,3},{3,4},{4,5},{5,6},{6,7},{8,9},{9,10},{10,11},{11... | collective-permute-start | bytes 2359304 | tf_op jit(solution)/shard_map/while/body/eval_jaxpr/ppermute | solution.py:27
  718.9 20.1 %collective-permute-start.1 = (bf16[2,128,1536]{2,1,0:T(8,128)(2,1)S(1)}, bf16[2,128,1536]{2,1,0:T(8,128)(2,1)S(1)}, u32[]{:S(2)}, u32[]{:S(2)}) collective-permute-start(bf16[2,128,1536]{2,1,0:T(8,128)(2,1)S(1)} %get-tuple-element.507), channel_id=1, source_target_pairs={{1,0},{2,1},{3,2},{4,3},{5,4},{6,5},{7,6},{9,8},{10,9},{11,10},{12... | collective-permute-start | bytes 2359304 | tf_op jit(solution)/shard_map/while/body/eval_jaxpr/ppermute | solution.py:29
  793.0 21.4 %collective-permute-start.2 = (bf16[128,1536]{1,0:T(8,128)(2,1)}, bf16[128,1536]{1,0:T(8,128)(2,1)S(1)}, u32[]{:S(2)}, u32[]{:S(2)}) collective-permute-start(bf16[128,1536]{1,0:T(8,128)(2,1)} %get-tuple-element.510), channel_id=1, source_target_pairs={{0,8},{8,16},{16,24},{1,9},{9,17},{17,25},{2,10},{10,18},{18,26},{... | collective-permute-start | bytes 1179656 | tf_op jit(solution)/shard_map/while/body/eval_jaxpr/ppermute | solution.py:39
  825.4 31.1 %collective-permute-start = (bf16[2,128,1536]{2,1,0:T(8,128)(2,1)S(1)}, bf16[2,128,1536]{2,1,0:T(8,128)(2,1)S(1)}, u32[]{:S(2)}, u32[]{:S(2)}) collective-permute-start(bf16[2,128,1536]{2,1,0:T(8,128)(2,1)S(1)} %get-tuple-element.507), channel_id=1, source_target_pairs={{0,1},{1,2},{2,3},{3,4},{4,5},{5,6},{6,7},{8,9},{9,10},{10,11},{11... | collective-permute-start | bytes 2359304 | tf_op jit(solution)/shard_map/while/body/eval_jaxpr/ppermute | solution.py:27
  827.3 37.2 %collective-permute-start.1 = (bf16[2,128,1536]{2,1,0:T(8,128)(2,1)S(1)}, bf16[2,128,1536]{2,1,0:T(8,128)(2,1)S(1)}, u32[]{:S(2)}, u32[]{:S(2)}) collective-permute-start(bf16[2,128,1536]{2,1,0:T(8,128)(2,1)S(1)} %get-tuple-element.507), channel_id=1, source_target_pairs={{1,0},{2,1},{3,2},{4,3},{5,4},{6,5},{7,6},{9,8},{10,9},{11,10},{12... | collective-permute-start | bytes 2359304 | tf_op jit(solution)/shard_map/while/body/eval_jaxpr/ppermute | solution.py:29
  918.4 3.8 collective-permute-start.2
  933.2 32.3 %collective-permute-start = (bf16[2,128,1536]{2,1,0:T(8,128)(2,1)S(1)}, bf16[2,128,1536]{2,1,0:T(8,128)(2,1)S(1)}, u32[]{:S(2)}, u32[]{:S(2)}) collective-permute-start(bf16[2,128,1536]{2,1,0:T(8,128)(2,1)S(1)} %get-tuple-element.507), channel_id=1, source_target_pairs={{0,1},{1,2},{2,3},{3,4},{4,5},{5,6},{6,7},{8,9},{9,10},{10,11},{11... | collective-permute-start | bytes 2359304 | tf_op jit(solution)/shard_map/while/body/eval_jaxpr/ppermute | solution.py:27
  935.1 33.7 %collective-permute-start.1 = (bf16[2,128,1536]{2,1,0:T(8,128)(2,1)S(1)}, bf16[2,128,1536]{2,1,0:T(8,128)(2,1)S(1)}, u32[]{:S(2)}, u32[]{:S(2)}) collective-permute-start(bf16[2,128,1536]{2,1,0:T(8,128)(2,1)S(1)} %get-tuple-element.507), channel_id=1, source_target_pairs={{1,0},{2,1},{3,2},{4,3},{5,4},{6,5},{7,6},{9,8},{10,9},{11,10},{12... | collective-permute-start | bytes 2359304 | tf_op jit(solution)/shard_map/while/body/eval_jaxpr/ppermute | solution.py:29
  1022.6 3.8 collective-permute-start.2
  (23 other events, 521.9 us)
Sparse Core Ops, SparseCore 0:
  9.5 153.6 all-gather.8
  165.4 77.7 all-gather.10
  245.4 78.0 all-gather.12
  325.5 78.0 all-gather.14
where the time goes:
time: 1040 us; the launch traced here: 1030 us
  waiting for transfers between devices  761 us (73%)
  local copies, waits for them, and re-layouts  124 us (12%)
  matrix products  52.2 us (5%)
  starting transfers between devices  51.1 us (5%)
  other arithmetic  30.1 us (3%)
  between operations  13.2 us (1%)
    ppermute x7, waiting for transfers between devices, extended(): lax.ppermute(tail, axis, [(i, (i + 1) % count) for i in range(ends)])  255 us
    ppermute x6, waiting for transfers between devices, from_behind(): return lax.ppermute(value, axis, pairs)  216 us
    all_gather x1, waiting for transfers between devices, per_device(): lax.all_gather(value_weight[0], 'seq', axis=0, tiled=True)  80.2 us
    all_gather x1, waiting for transfers between devices, per_device(): lax.all_gather(out_weight[0], 'seq', axis=0, tiled=True)  80.1 us
    all_gather x1, waiting for transfers between devices, per_device(): lax.all_gather(key_weight[0], 'seq', axis=0, tiled=True)  80 us
    ppermute x7, waiting for transfers between devices, extended(): lax.ppermute(head, axis, [((i + 1) % count, i) for i in range(ends)])  33.2 us
    ppermute x7, starting transfers between devices, extended(): lax.ppermute(head, axis, [((i + 1) % count, i) for i in range(ends)])  28.3 us
  transfers between devices with their start and end apart: 24, of which 24 were waited for; matrix products, arithmetic and copies ran while one was open for 1% of the time, Pallas kernels for 0%

commit v1 on v0

v1 whole, which is shorter than its diff:
```python
import functools
import math

import jax
import jax.numpy as jnp
from jax import lax
from jax.experimental import pallas as pl
from jax.experimental.pallas import tpu as pltpu
from jax.sharding import PartitionSpec as P

D = 1536
HEADS = 12
HEAD = 128
TILE = 64
PATCHES = 3
TPP = 2
TPD = PATCHES * TPP
WIDE = 256
CHUNKS = D // WIDE
LANE_CHUNKS = CHUNKS // 2
MATS = 4
EPSILON = 1e-06
MESH = pl.DeviceIdType.MESH


def head_normed(projected, gain):
    mean = jnp.mean(projected * projected, axis=-1, keepdims=True)
    return (projected * lax.rsqrt(mean + EPSILON) * gain).astype(jnp.bfloat16)


def ring_place(seq, n):
    half = seq // 2
    return jnp.where(seq % 2 == 0, half, n - 1 - half)


def ring_seq(place, n):
    return jnp.where(place < n // 2, 2 * place, 2 * (n - 1 - place) + 1)


def kernel(
    n_seg,
    n_seq,
    tidx_ref,
    listed_ref,
    gain_q_ref,
    gain_k_ref,
    latent_ref,
    stale_ref,
    wq_ref,
    wk_ref,
    wv_ref,
    wo_ref,
    out_ref,
    weights,
    kv,
    xbuf,
    attn,
    load_sem,
    own_sem,
    ring_send,
    ring_recv,
    stale_send,
    stale_recv,
    x_send,
    x_recv,
):
    seg = lax.axis_index("segment")
    seq = lax.axis_index("seq")
    depth = wq_ref.shape[0]
    patch_rows = xbuf.shape[2]
    has_left = seq > 0
    has_right = seq < n_seq - 1
    has_next = seg < n_seg - 1
    has_prev = seg > 0
    place = ring_place(seq, n_seq)
    ring_right = ring_seq(lax.rem(place + 1, n_seq), n_seq)
    ring_left = ring_seq(lax.rem(place + n_seq - 1, n_seq), n_seq)

    mine = pl.ds(pl.multiple_of(seq * depth, 16), depth)
    loads = []
    for mat, ref in enumerate((wq_ref, wk_ref, wv_ref, wo_ref)):
        for c in range(CHUNKS):
            loads.append(
                pltpu.make_async_copy(
                    ref.at[:, pl.ds(c * WIDE, WIDE)],
                    weights.at[c, mat, mine, :],
                    load_sem.at[mat * CHUNKS + c],
                )
            )
    for load in loads:
        load.start()
    own_stale = pltpu.make_async_copy(
        stale_ref.at[:, pl.ds(TPP, TPD - TPP)],
        kv.at[:, pl.ds(TPD + TPP, TPD - TPP)],
        own_sem,
    )
    own_stale.start()

    @pl.when(jnp.logical_not(has_left))
    def _():
        xbuf[:, 0] = jnp.zeros((PATCHES, patch_rows, D), jnp.bfloat16)

    @pl.when(jnp.logical_not(has_right))
    def _():
        xbuf[:, 2] = jnp.zeros((PATCHES, patch_rows, D), jnp.bfloat16)

    @pl.when(seg == 0)
    def _():
        xbuf[:, 1] = latent_ref[...]

    barrier = pltpu.get_barrier_semaphore()
    sides = ((-1, has_left), (0, None), (1, has_right))

    def greet(to_seg, to_seq):
        pl.semaphore_signal(barrier, inc=1, device_id=(to_seg, to_seq), device_id_type=MESH)

    greet(seg, ring_right)
    greet(seg, ring_left)
    pl.when(has_left)(lambda: greet(seg, seq - 1))
    pl.when(has_right)(lambda: greet(seg, seq + 1))
    for by, there in sides:
        ahead = has_next if there is None else jnp.logical_and(has_next, there)
        behind = has_prev if there is None else jnp.logical_and(has_prev, there)
        pl.when(ahead)(functools.partial(greet, seg + 1, seq + by))
        pl.when(behind)(functools.partial(greet, seg - 1, seq + by))
    beside = has_left.astype(jnp.int32) + has_right.astype(jnp.int32)
    levels = has_next.astype(jnp.int32) + has_prev.astype(jnp.int32)
    pl.semaphore_wait(barrier, 2 + beside + levels * (1 + beside))

    def x_copy(src, patch, by, to_seg):
        return pltpu.make_async_remote_copy(
            src_ref=src.at[patch],
            dst_ref=xbuf.at[patch, 1 - by],
            send_sem=x_send.at[patch, 1 - by],
            recv_sem=x_recv.at[patch, 1 - by],
            device_id=(to_seg, seq + by),
            device_id_type=MESH,
        )

    def stale_copy(by):
        return pltpu.make_async_remote_copy(
            src_ref=stale_ref.at[:, pl.ds(TPP, TPD - TPP)],
            dst_ref=kv.at[:, pl.ds((1 - by) * TPD + TPP, TPD - TPP)],
            send_sem=stale_send.at[1 - by],
            recv_sem=stale_recv.at[1 - by],
            device_id=(seg, seq + by),
            device_id_type=MESH,
        )

    def ring_copy(step, way, part):
        owner = lax.rem(place + (n_seq - step if way == 0 else step), n_seq)
        rows = pl.ds(pl.multiple_of(ring_seq(owner, n_seq) * depth, 16), depth)
        block = weights.at[way * LANE_CHUNKS + part, :, rows, :]
        return pltpu.make_async_remote_copy(
            src_ref=block,
            dst_ref=block,
            send_sem=ring_send.at[way, step, part],
            recv_sem=ring_recv.at[way, step, part],
            device_id=(seg, ring_right if way == 0 else ring_left),
            device_id_type=MESH,
        )

    def ring_arrival(step, way, part):
        owner = lax.rem(place + (n_seq - step - 1 if way == 0 else step + 1), n_seq)
        rows = pl.ds(pl.multiple_of(ring_seq(owner, n_seq) * depth, 16), depth)
        block = weights.at[way * LANE_CHUNKS + part, :, rows, :]
        return pltpu.make_async_remote_copy(
            src_ref=block,
            dst_ref=block,
            send_sem=ring_send.at[way, step, part],
            recv_sem=ring_recv.at[way, step, part],
            device_id=(seg, ring_right if way == 0 else ring_left),
            device_id_type=MESH,
        )

    parts = [(part, way) for part in range(LANE_CHUNKS) for way in range(2)]
    for load in loads:
        load.wait()
    for part, way in parts:
        ring_copy(0, way, part).start()

    def send_latent(patch, carry):
        pl.when(has_left)(lambda: x_copy(latent_ref, patch, -1, seg).start())
        pl.when(has_right)(lambda: x_copy(latent_ref, patch, 1, seg).start())
        return carry

    @pl.when(seg == 0)
    def _():
        lax.fori_loop(0, PATCHES, send_latent, 0)

    pl.when(has_left)(lambda: stale_copy(-1).start())
    pl.when(has_right)(lambda: stale_copy(1).start())

    def forward(step, carry):
        for part, way in parts:
            ring_arrival(step - 1, way, part).wait_recv()
            ring_copy(step, way, part).start()
        return carry

    lax.fori_loop(1, n_seq - 1, forward, 0)
    for part, way in parts:
        ring_arrival(n_seq - 2, way, part).wait_recv()

    own_stale.wait()
    pl.when(has_left)(lambda: stale_copy(1).wait_recv())
    pl.when(has_right)(lambda: stale_copy(-1).wait_recv())

    gain_q = gain_q_ref[...]
    gain_k = gain_k_ref[...]

    def do_patch(patch, carry):
        pl.when(has_left)(lambda: x_copy(out_ref, patch, 1, seg).wait_recv())
        pl.when(has_right)(lambda: x_copy(out_ref, patch, -1, seg).wait_recv())
        pl.when(has_prev)(lambda: x_copy(out_ref, patch, 0, seg).wait_recv())

        def do_heads(c, inner):
            columns = pl.ds(pl.multiple_of(c * WIDE, WIDE), WIDE)
            rows3 = xbuf[patch].reshape(3 * patch_rows, D)
            q = jnp.dot(xbuf[patch, 1], weights[c, 0], preferred_element_type=jnp.float32)
            k = jnp.dot(rows3, weights[c, 1], preferred_element_type=jnp.float32)
            v = jnp.dot(rows3, weights[c, 2], preferred_element_type=jnp.float32)
            fresh_q, fresh_k = [], []
            for h in range(WIDE // HEAD):
                lanes = slice(h * HEAD, (h + 1) * HEAD)
                fresh_q.append(head_normed(q[:, lanes], gain_q))
                fresh_k.append(head_normed(k[:, lanes], gain_k))
            fresh_k = jnp.concatenate(fresh_k, axis=1).reshape(3, TPP, TILE, WIDE)
            fresh_v = v.astype(jnp.bfloat16).reshape(3, TPP, TILE, WIDE)
            for f in range(3):
                tiles = pl.ds(f * TPD + patch * TPP, TPP)
                kv[0, tiles, :, columns] = fresh_k[f]
                kv[1, tiles, :, columns] = fresh_v[f]
            for i in range(TPP):
                g = patch * TPP + i
                places = [tidx_ref[g, m] for m in range(TPD)]
                listed = listed_ref[g]
                keys = jnp.concatenate([kv[0, t, :, columns] for t in places], axis=0)
                values = jnp.concatenate([kv[1, t, :, columns] for t in places], axis=0)
                for h in range(WIDE // HEAD):
                    lanes = slice(h * HEAD, (h + 1) * HEAD)
                    score = lax.dot_general(
                        fresh_q[h][i * TILE : (i + 1) * TILE],
                        keys[:, lanes],
                        (((1,), (1,)), ((), ())),
                        preferred_element_type=jnp.float32,
                    )
                    weight = jnp.exp(score * (1.0 / math.sqrt(HEAD))) * listed
                    total = jnp.sum(weight, axis=-1, keepdims=True)
                    summed = jnp.dot(
                        weight.astype(jnp.bfloat16),
                        values[:, lanes],
                        preferred_element_type=jnp.float32,
                    )
                    spot = pl.ds(pl.multiple_of(c * WIDE + h * HEAD, HEAD), HEAD)
                    attn[i * TILE : (i + 1) * TILE, spot] = (summed / total).astype(jnp.bfloat16)
            return inner

        lax.fori_loop(0, CHUNKS, do_heads, 0)

        def do_out(c, inner):
            columns = pl.ds(pl.multiple_of(c * WIDE, WIDE), WIDE)
            mixed = jnp.dot(attn[...], weights[c, 3], preferred_element_type=jnp.float32)
            entering = xbuf[patch, 1, :, columns].astype(jnp.float32)
            out_ref[patch, :, columns] = (entering + mixed).astype(jnp.bfloat16)
            return inner

        lax.fori_loop(0, CHUNKS, do_out, 0)

        @pl.when(has_next)
        def _():
            x_copy(out_ref, patch, 0, seg + 1).start()
            pl.when(has_left)(lambda: x_copy(out_ref, patch, -1, seg + 1).start())
            pl.when(has_right)(lambda: x_copy(out_ref, patch, 1, seg + 1).start())

        return carry

    def latent_left(patch, carry):
        pl.when(has_left)(lambda: x_copy(latent_ref, patch, -1, seg).wait_send())
        pl.when(has_right)(lambda: x_copy(latent_ref, patch, 1, seg).wait_send())
        return carry

    @pl.when(seg == 0)
    def _():
        lax.fori_loop(0, PATCHES, latent_left, 0)

    lax.fori_loop(0, PATCHES, do_patch, 0)

    def drain_ring(step, carry):
        for part, way in parts:
            ring_copy(step, way, part).wait_send()
        return carry

    lax.fori_loop(0, n_seq - 1, drain_ring, 0)
    pl.when(has_left)(lambda: stale_copy(-1).wait_send())
    pl.when(has_right)(lambda: stale_copy(1).wait_send())

    def drain_x(patch, carry):
        x_copy(out_ref, patch, 0, seg + 1).wait_send()
        pl.when(has_left)(lambda: x_copy(out_ref, patch, -1, seg + 1).wait_send())
        pl.when(has_right)(lambda: x_copy(out_ref, patch, 1, seg + 1).wait_send())
        return carry

    @pl.when(has_next)
    def _():
        lax.fori_loop(0, PATCHES, drain_x, 0)


def per_device(
    n_seg,
    n_seq,
    latent,
    stale_kv,
    query_weight,
    key_weight,
    value_weight,
    out_weight,
    query_gain,
    key_gain,
    tile_mask,
):
    tok_dev = latent.shape[0]
    patch_rows = tok_dev // PATCHES
    tiles_dev = tile_mask.shape[0]
    seq = lax.axis_index("seq")
    usable = tile_mask >= 0
    own = tiles_dev + jnp.arange(tiles_dev, dtype=jnp.int32)[:, None]
    tidx = jnp.where(usable, tile_mask - (seq - 1) * tiles_dev, own)
    listed = jnp.repeat(usable, TILE, axis=1).astype(jnp.float32)[:, None, :]
    vmem = pl.BlockSpec(memory_space=pltpu.VMEM)
    smem = pl.BlockSpec(memory_space=pltpu.SMEM)
    anywhere = pl.BlockSpec(memory_space=pl.ANY)
    steps = n_seq - 1
    dma = pltpu.SemaphoreType.DMA
    result = pl.pallas_call(
        functools.partial(kernel, n_seg, n_seq),
        out_shape=jax.ShapeDtypeStruct((PATCHES, patch_rows, D), jnp.bfloat16),
        in_specs=[smem, vmem, vmem, vmem, vmem] + [anywhere] * 5,
        out_specs=vmem,
        scratch_shapes=[
            pltpu.VMEM((CHUNKS, MATS, D, WIDE), jnp.bfloat16),
            pltpu.VMEM((2, 3 * tiles_dev, TILE, D), jnp.bfloat16),
            pltpu.VMEM((PATCHES, 3, patch_rows, D), jnp.bfloat16),
            pltpu.VMEM((patch_rows, D), jnp.bfloat16),
            dma((MATS * CHUNKS,)),
            dma,
            dma((2, steps, LANE_CHUNKS)),
            dma((2, steps, LANE_CHUNKS)),
            dma((3,)),
            dma((3,)),
            dma((PATCHES, 3)),
            dma((PATCHES, 3)),
        ],
        compiler_params=pltpu.CompilerParams(
            collective_id=0, has_side_effects=True, vmem_limit_bytes=56 * 1024 * 1024
        ),
    )(
        tidx,
        listed,
        query_gain,
        key_gain,
        latent.reshape(PATCHES, patch_rows, D),
        stale_kv[0].reshape(2, tiles_dev, TILE, D),
        query_weight[0],
        key_weight[0],
        value_weight[0],
        out_weight[0],
    )
    return result.reshape(1, tok_dev, D)


def solution(mesh):
    return jax.shard_map(
        functools.partial(per_device, mesh.shape["segment"], mesh.shape["seq"]),
        mesh=mesh,
        in_specs=(
            P("seq", None),
            P("segment", None, "seq", None),
            P("segment", "seq", None),
            P("segment", "seq", None),
            P("segment", "seq", None),
            P("segment", "seq", None),
            P("segment", None),
            P("segment", None),
            P("seq", None),
        ),
        out_specs=P("segment", "seq", None),
        check_vma=False,
    )
```

time: 1040 us -> 406 us (0.39)
  waiting for transfers between devices: 761 us -> 0 us
  Pallas kernels: 0 us -> 395 us
  local copies, waits for them, and re-layouts: 124 us -> 3.12 us
  matrix products: 52.2 us -> 0 us
  starting transfers between devices: 51.1 us -> 0 us
  other arithmetic: 30.1 us -> 2.04 us
  between operations: 13.2 us -> 0.01 us
    ppermute x20 -> x0, waiting for transfers between devices: 505 us -> none  [the longest x7 255 us: extended(): lax.ppermute(tail, axis, [(i, (i + 1) % count) for i in range(ends)])]
    pallas_call x0 -> x1, Pallas kernels: none -> 395 us  [per_device(): pl.pallas_call(functools.partial(kernel, n_seg, n_seq), out_shape=jax.Sha...]
    all_gather x4 -> x0, waiting for transfers between devices: 254 us -> none  [the longest x1 80.2 us: per_device(): lax.all_gather(value_weight[0], 'seq', axis=0, tiled=True)]
    dot_general x18 -> x0, matrix products: 52.2 us -> none  [the longest x3 14.2 us: attend(): jnp.einsum('pthe,pkhe->phtk', query_heads, key_heads, preferred_element_t...]
    ppermute x20 -> x0, starting transfers between devices: 51 us -> none  [the longest x7 28.3 us: extended(): lax.ppermute(head, axis, [((i + 1) % count, i) for i in range(ends)])]
    dynamic_update_slice x12 -> x0, local copies, waits for them, and re-layouts: 49.6 us -> none  [the longest x3 13.9 us: finish(): updated = lax.dynamic_update_slice_in_dim(former, trailing, offset, 1)]
    reshape x9 -> x0, local copies, waits for them, and re-layouts: 26.4 us -> none  [the longest x3 16.4 us: attend(): jnp.take(blocks[0], tile_index, axis=0).reshape(n_query, -1, HEADS, HEAD)]
    gather x6 -> x0, local copies, waits for them, and re-layouts: 18.9 us -> none  [the longest x3 12.4 us: attend(): jnp.take(blocks[1], tile_index, axis=0).reshape(n_query, -1, HEADS, HEAD)]
  transfers between devices with their start and end apart: 24 -> 0, of which waited for: 24 -> 0; matrix products, arithmetic and copies ran while one was open for 1% -> 0% of each run, Pallas kernels for 0% -> 0%
where the time goes in v1:
time: 406 us; the launch traced here: 400 us
  Pallas kernels  395 us (97%)
    pallas_call x1, Pallas kernels, per_device(): pl.pallas_call(functools.partial(kernel, n_seg, n_seq), out_shape=jax.Sha...  395 us

profile of v1, /device:TPU:19, one launch (start us, length us, event | category | flops | bytes accessed | tf_op | source)
XLA Modules:
  0.0 400.1 jit_solution(4788397172407341014)
XLA Ops:
  0.0 1.3 subtract_select_fusion.tidx_ref
  1.4 0.7 fusion
  2.0 0.1 broadcast_in_dim.14
  2.1 0.7 convert_element_type.15.listed_ref
  2.8 394.9 %shard_map.91 = bf16[3,128,1536]{2,1,0:T(8,128)(2,1)} custom-call(s32[6,6]{1,0:T(8,128)} %subtract_select_fusion.tidx_ref, f32[6,1,384]{2,1,0:T(1,128)} %convert_element_type.15.listed_ref, f32[1,128]{1,0:T(1,128)} %gain_q_ref.1, f32[1,128]{1,0:T(1,128)} %gain_k_ref.1, bf16[3,128,1536]{2,1,0:T(8,128)(2,1)} %bitcast.9, bf16[2,6,64,1536]{3,2,1,0:T(8,128)(2,1)} %bitcast.8, ...), custom_call_target="tpu_custom_call" | custom-call | tf_op jit(solution)/shard_map/pallas_call | solution.py:334
  397.7 2.4 copy.11
  (1 shorter events, 0.0 us)

commit v2 on v1

--- a/solution.py
+++ b/solution.py
@@ -59,6 +59,9 @@
     own_sem,
     ring_send,
     ring_recv,
+    last_send,
+    last_recv,
+    go_sem,
     stale_send,
     stale_recv,
     x_send,
@@ -147,37 +150,34 @@
             device_id_type=MESH,
         )
 
-    def ring_copy(step, way, part):
-        owner = lax.rem(place + (n_seq - step if way == 0 else step), n_seq)
-        rows = pl.ds(pl.multiple_of(ring_seq(owner, n_seq) * depth, 16), depth)
-        block = weights.at[way * LANE_CHUNKS + part, :, rows, :]
+    def ring_send_to(way, block, send_sem, recv_sem):
         return pltpu.make_async_remote_copy(
             src_ref=block,
             dst_ref=block,
-            send_sem=ring_send.at[way, step, part],
-            recv_sem=ring_recv.at[way, step, part],
+            send_sem=send_sem,
+            recv_sem=recv_sem,
             device_id=(seg, ring_right if way == 0 else ring_left),
             device_id_type=MESH,
         )
 
-    def ring_arrival(step, way, part):
-        owner = lax.rem(place + (n_seq - step - 1 if way == 0 else step + 1), n_seq)
-        rows = pl.ds(pl.multiple_of(ring_seq(owner, n_seq) * depth, 16), depth)
-        block = weights.at[way * LANE_CHUNKS + part, :, rows, :]
-        return pltpu.make_async_remote_copy(
-            src_ref=block,
-            dst_ref=block,
-            send_sem=ring_send.at[way, step, part],
-            recv_sem=ring_recv.at[way, step, part],
-            device_id=(seg, ring_right if way == 0 else ring_left),
-            device_id_type=MESH,
-        )
+    def ring_rows(step, way, late):
+        owner = lax.rem(place + (n_seq - step - late if way == 0 else step + late), n_seq)
+        return pl.ds(pl.multiple_of(ring_seq(owner, n_seq) * depth, 16), depth)
+
+    def ring_copy(step, way, part, late=0):
+        rows = ring_rows(step, way, late)
+        block = weights.at[way * LANE_CHUNKS + part, pl.ds(0, MATS - 1), rows, :]
+        return ring_send_to(way, block, ring_send.at[way, step, part], ring_recv.at[way, step, part])
+
+    def last_copy(step, way, late=0):
+        rows = ring_rows(step, way, late)
+        block = weights.at[pl.ds(way * LANE_CHUNKS, LANE_CHUNKS), MATS - 1, rows, :]
+        return ring_send_to(way, block, last_send.at[way, step], last_recv.at[way, step])
 
     parts = [(part, way) for part in range(LANE_CHUNKS) for way in range(2)]
+    odd = lax.rem(seg, 2) == 1
     for load in loads:
         load.wait()
-    for part, way in parts:
-        ring_copy(0, way, part).start()
 
     def send_latent(patch, carry):
         pl.when(has_left)(lambda: x_copy(latent_ref, patch, -1, seg).start())
@@ -191,15 +191,43 @@
     pl.when(has_left)(lambda: stale_copy(-1).start())
     pl.when(has_right)(lambda: stale_copy(1).start())
 
+    pl.when(odd)(lambda: pl.semaphore_wait(go_sem, 1))
+    for part, way in parts:
+        ring_copy(0, way, part).start()
+
     def forward(step, carry):
         for part, way in parts:
-            ring_arrival(step - 1, way, part).wait_recv()
+            ring_copy(step - 1, way, part, 1).wait_recv()
             ring_copy(step, way, part).start()
         return carry
 
     lax.fori_loop(1, n_seq - 1, forward, 0)
+    for way in range(2):
+        last_copy(0, way).start()
     for part, way in parts:
-        ring_arrival(n_seq - 2, way, part).wait_recv()
+        ring_copy(n_seq - 2, way, part, 1).wait_recv()
+
+    @pl.when(jnp.logical_not(odd))
+    def _():
+        pl.semaphore_signal(go_sem, inc=1, device_id=(seg + 1, seq), device_id_type=MESH)
+
+    def forward_last(step, carry):
+        for way in range(2):
+            last_copy(step - 1, way, 1).wait_recv()
+            last_copy(step, way).start()
+        return carry
+
+    def finish_last():
+        for way in range(2):
+            last_copy(n_seq - 2, way, 1).wait_recv()
+
+    early = seg < 2
+    per_chunk = pl.cdiv(n_seq - 2, CHUNKS)
+
+    @pl.when(jnp.logical_not(early))
+    def _():
+        lax.fori_loop(1, n_seq - 1, forward_last, 0)
+        finish_last()
 
     own_stale.wait()
     pl.when(has_left)(lambda: stale_copy(1).wait_recv())
@@ -213,7 +241,15 @@
         pl.when(has_right)(lambda: x_copy(out_ref, patch, -1, seg).wait_recv())
         pl.when(has_prev)(lambda: x_copy(out_ref, patch, 0, seg).wait_recv())
 
+        beside_last = jnp.logical_and(early, patch == 0)
+
         def do_heads(c, inner):
+            @pl.when(beside_last)
+            def _():
+                first = 1 + c * per_chunk
+                until = jnp.minimum(first + per_chunk, n_seq - 1)
+                lax.fori_loop(first, until, forward_last, 0)
+
             columns = pl.ds(pl.multiple_of(c * WIDE, WIDE), WIDE)
             rows3 = xbuf[patch].reshape(3 * patch_rows, D)
             q = jnp.dot(xbuf[patch, 1], weights[c, 0], preferred_element_type=jnp.float32)
@@ -257,6 +293,8 @@
 
         lax.fori_loop(0, CHUNKS, do_heads, 0)
 
+        pl.when(beside_last)(finish_last)
+
         def do_out(c, inner):
             columns = pl.ds(pl.multiple_of(c * WIDE, WIDE), WIDE)
             mixed = jnp.dot(attn[...], weights[c, 3], preferred_element_type=jnp.float32)
@@ -268,9 +306,9 @@
 
         @pl.when(has_next)
         def _():
-            x_copy(out_ref, patch, 0, seg + 1).start()
             pl.when(has_left)(lambda: x_copy(out_ref, patch, -1, seg + 1).start())
             pl.when(has_right)(lambda: x_copy(out_ref, patch, 1, seg + 1).start())
+            x_copy(out_ref, patch, 0, seg + 1).start()
 
         return carry
 
@@ -288,6 +326,8 @@
     def drain_ring(step, carry):
         for part, way in parts:
             ring_copy(step, way, part).wait_send()
+        for way in range(2):
+            last_copy(step, way).wait_send()
         return carry
 
     lax.fori_loop(0, n_seq - 1, drain_ring, 0)
@@ -345,6 +385,9 @@
             dma,
             dma((2, steps, LANE_CHUNKS)),
             dma((2, steps, LANE_CHUNKS)),
+            dma((2, steps)),
+            dma((2, steps)),
+            pltpu.SemaphoreType.REGULAR,
             dma((3,)),
             dma((3,)),
             dma((PATCHES, 3)),

time: 406 us -> 406 us (level); the launches traced: 400 us -> 406 us
  Pallas kernels: 395 us -> 401 us
    pallas_call x1, Pallas kernels: 395 us -> 401 us  [per_device(): pl.pallas_call(functools.partial(kernel, n_seg, n_seq), out_shape=jax.Sha...]
where the time goes in v2:
time: 406 us
  Pallas kernels  401 us (99%)
    pallas_call x1, Pallas kernels, per_device(): pl.pallas_call(functools.partial(kernel, n_seg, n_seq), out_shape=jax.Sha...  401 us

profile of v2, /device:TPU:19, one launch (start us, length us, event | category | flops | bytes accessed | tf_op | source)
XLA Modules:
  0.0 405.8 jit_solution(12793088723233001083)
XLA Ops:
  0.0 1.3 subtract_select_fusion.tidx_ref
  1.4 0.7 fusion
  2.0 0.1 broadcast_in_dim.14
  2.1 0.7 convert_element_type.15.listed_ref
  2.8 400.6 %shard_map.91 = bf16[3,128,1536]{2,1,0:T(8,128)(2,1)} custom-call(s32[6,6]{1,0:T(8,128)} %subtract_select_fusion.tidx_ref, f32[6,1,384]{2,1,0:T(1,128)} %convert_element_type.15.listed_ref, f32[1,128]{1,0:T(1,128)} %gain_q_ref.1, f32[1,128]{1,0:T(1,128)} %gain_k_ref.1, bf16[3,128,1536]{2,1,0:T(8,128)(2,1)} %bitcast.9, bf16[2,6,64,1536]{3,2,1,0:T(8,128)(2,1)} %bitcast.8, ...), custom_call_target="tpu_custom_call" | custom-call | tf_op jit(solution)/shard_map/pallas_call | solution.py:374
  403.4 2.4 copy.11
  (1 shorter events, 0.0 us)

commit v3 on v2

--- a/solution.py
+++ b/solution.py
@@ -55,6 +55,9 @@
     kv,
     xbuf,
     attn,
+    queries,
+    fresh_q,
+    fresh,
     load_sem,
     own_sem,
     ring_send,
@@ -188,17 +191,21 @@
     def _():
         lax.fori_loop(0, PATCHES, send_latent, 0)
 
-    pl.when(has_left)(lambda: stale_copy(-1).start())
-    pl.when(has_right)(lambda: stale_copy(1).start())
-
     pl.when(odd)(lambda: pl.semaphore_wait(go_sem, 1))
     for part, way in parts:
         ring_copy(0, way, part).start()
+    pl.when(has_left)(lambda: stale_copy(-1).start())
+    pl.when(has_right)(lambda: stale_copy(1).start())
 
     def forward(step, carry):
         for part, way in parts:
             ring_copy(step - 1, way, part, 1).wait_recv()
             ring_copy(step, way, part).start()
+
+        @pl.when(jnp.logical_and(step == n_seq // 2 - 1, jnp.logical_not(odd)))
+        def _():
+            pl.semaphore_signal(go_sem, inc=1, device_id=(seg + 1, seq), device_id_type=MESH)
+
         return carry
 
     lax.fori_loop(1, n_seq - 1, forward, 0)
@@ -207,10 +214,6 @@
     for part, way in parts:
         ring_copy(n_seq - 2, way, part, 1).wait_recv()
 
-    @pl.when(jnp.logical_not(odd))
-    def _():
-        pl.semaphore_signal(go_sem, inc=1, device_id=(seg + 1, seq), device_id_type=MESH)
-
     def forward_last(step, carry):
         for way in range(2):
             last_copy(step - 1, way, 1).wait_recv()
@@ -243,39 +246,41 @@
 
         beside_last = jnp.logical_and(early, patch == 0)
 
-        def do_heads(c, inner):
-            @pl.when(beside_last)
-            def _():
-                first = 1 + c * per_chunk
-                until = jnp.minimum(first + per_chunk, n_seq - 1)
-                lax.fori_loop(first, until, forward_last, 0)
-
-            columns = pl.ds(pl.multiple_of(c * WIDE, WIDE), WIDE)
+        def project(c):
             rows3 = xbuf[patch].reshape(3 * patch_rows, D)
-            q = jnp.dot(xbuf[patch, 1], weights[c, 0], preferred_element_type=jnp.float32)
             k = jnp.dot(rows3, weights[c, 1], preferred_element_type=jnp.float32)
-            v = jnp.dot(rows3, weights[c, 2], preferred_element_type=jnp.float32)
-            fresh_q, fresh_k = [], []
             for h in range(WIDE // HEAD):
                 lanes = slice(h * HEAD, (h + 1) * HEAD)
-                fresh_q.append(head_normed(q[:, lanes], gain_q))
-                fresh_k.append(head_normed(k[:, lanes], gain_k))
-            fresh_k = jnp.concatenate(fresh_k, axis=1).reshape(3, TPP, TILE, WIDE)
-            fresh_v = v.astype(jnp.bfloat16).reshape(3, TPP, TILE, WIDE)
+                fresh[0, :, lanes] = head_normed(k[:, lanes], gain_k)
+            v = jnp.dot(rows3, weights[c, 2], preferred_element_type=jnp.float32)
+            fresh[1] = v.astype(jnp.bfloat16)
+            q = jnp.dot(xbuf[patch, 1], weights[c, 0], preferred_element_type=jnp.float32)
+            for h in range(WIDE // HEAD):
+                lanes = slice(h * HEAD, (h + 1) * HEAD)
+                fresh_q[:, lanes] = head_normed(q[:, lanes], gain_q)
+
+        def keep(c):
+            columns = pl.ds(pl.multiple_of(c * WIDE, WIDE), WIDE)
+            queries[...] = fresh_q[...]
             for f in range(3):
                 tiles = pl.ds(f * TPD + patch * TPP, TPP)
-                kv[0, tiles, :, columns] = fresh_k[f]
-                kv[1, tiles, :, columns] = fresh_v[f]
+                rows = slice(f * patch_rows, (f + 1) * patch_rows)
+                for which in range(2):
+                    kv[which, tiles, :, columns] = fresh[which, rows].reshape(TPP, TILE, WIDE)
+
+        def attend(c):
+            columns = pl.ds(pl.multiple_of(c * WIDE, WIDE), WIDE)
             for i in range(TPP):
                 g = patch * TPP + i
                 places = [tidx_ref[g, m] for m in range(TPD)]
                 listed = listed_ref[g]
                 keys = jnp.concatenate([kv[0, t, :, columns] for t in places], axis=0)
                 values = jnp.concatenate([kv[1, t, :, columns] for t in places], axis=0)
+                own = queries[i * TILE : (i + 1) * TILE, :]
                 for h in range(WIDE // HEAD):
                     lanes = slice(h * HEAD, (h + 1) * HEAD)
                     score = lax.dot_general(
-                        fresh_q[h][i * TILE : (i + 1) * TILE],
+                        own[:, lanes],
                         keys[:, lanes],
                         (((1,), (1,)), ((), ())),
                         preferred_element_type=jnp.float32,
@@ -289,9 +294,21 @@
                     )
                     spot = pl.ds(pl.multiple_of(c * WIDE + h * HEAD, HEAD), HEAD)
                     attn[i * TILE : (i + 1) * TILE, spot] = (summed / total).astype(jnp.bfloat16)
+
+        def do_heads(c, inner):
+            @pl.when(beside_last)
+            def _():
+                first = 1 + c * per_chunk
+                until = jnp.minimum(first + per_chunk, n_seq - 1)
+                lax.fori_loop(first, until, forward_last, 0)
+
+            ahead = jnp.minimum(c, CHUNKS - 1)
+            project(ahead)
+            attend(jnp.maximum(c - 1, 0))
+            keep(ahead)
             return inner
 
-        lax.fori_loop(0, CHUNKS, do_heads, 0)
+        lax.fori_loop(0, CHUNKS + 1, do_heads, 0)
 
         pl.when(beside_last)(finish_last)
 
@@ -381,6 +398,9 @@
             pltpu.VMEM((2, 3 * tiles_dev, TILE, D), jnp.bfloat16),
             pltpu.VMEM((PATCHES, 3, patch_rows, D), jnp.bfloat16),
             pltpu.VMEM((patch_rows, D), jnp.bfloat16),
+            pltpu.VMEM((patch_rows, WIDE), jnp.bfloat16),
+            pltpu.VMEM((patch_rows, WIDE), jnp.bfloat16),
+            pltpu.VMEM((2, 3 * patch_rows, WIDE), jnp.bfloat16),
             dma((MATS * CHUNKS,)),
             dma,
             dma((2, steps, LANE_CHUNKS)),

time: 406 us -> 403 us (level)
  Pallas kernels: 401 us -> 395 us
    pallas_call x1, Pallas kernels: 401 us -> 395 us  [per_device(): pl.pallas_call(functools.partial(kernel, n_seg, n_seq), out_shape=jax.Sha...]
where the time goes in v3:
time: 403 us; the launch traced here: 400 us
  Pallas kernels  395 us (98%)
    pallas_call x1, Pallas kernels, per_device(): pl.pallas_call(functools.partial(kernel, n_seg, n_seq), out_shape=jax.Sha...  395 us

profile of v3, /device:TPU:19, one launch (start us, length us, event | category | flops | bytes accessed | tf_op | source)
XLA Modules:
  0.0 400.4 jit_solution(11075222903902026989)
XLA Ops:
  0.0 1.3 subtract_select_fusion.tidx_ref
  1.4 0.7 fusion
  2.0 0.1 broadcast_in_dim.14
  2.1 0.7 convert_element_type.15.listed_ref
  2.8 395.2 %shard_map.91 = bf16[3,128,1536]{2,1,0:T(8,128)(2,1)} custom-call(s32[6,6]{1,0:T(8,128)} %subtract_select_fusion.tidx_ref, f32[6,1,384]{2,1,0:T(1,128)} %convert_element_type.15.listed_ref, f32[1,128]{1,0:T(1,128)} %gain_q_ref.1, f32[1,128]{1,0:T(1,128)} %gain_k_ref.1, bf16[3,128,1536]{2,1,0:T(8,128)(2,1)} %bitcast.9, bf16[2,6,64,1536]{3,2,1,0:T(8,128)(2,1)} %bitcast.8, ...), custom_call_target="tpu_custom_call" | custom-call | tf_op jit(solution)/shard_map/pallas_call | solution.py:391
  398.0 2.4 copy.11
  (1 shorter events, 0.0 us)

commit v4 on v3

--- a/solution.py
+++ b/solution.py
@@ -131,7 +131,12 @@
         pl.when(behind)(functools.partial(greet, seg - 1, seq + by))
     beside = has_left.astype(jnp.int32) + has_right.astype(jnp.int32)
     levels = has_next.astype(jnp.int32) + has_prev.astype(jnp.int32)
-    pl.semaphore_wait(barrier, 2 + beside + levels * (1 + beside))
+    two_left = seq >= 2
+    two_right = seq < n_seq - 2
+    pl.when(two_left)(lambda: greet(seg, seq - 2))
+    pl.when(two_right)(lambda: greet(seg, seq + 2))
+    farther = two_left.astype(jnp.int32) + two_right.astype(jnp.int32)
+    pl.semaphore_wait(barrier, 2 + beside + farther + levels * (1 + beside))
 
     def x_copy(src, patch, by, to_seg):
         return pltpu.make_async_remote_copy(
@@ -143,13 +148,31 @@
             device_id_type=MESH,
         )
 
-    def stale_copy(by):
+    toward = jnp.where(lax.rem(seq, 2) == 0, 1, -1)
+    hands_on = jnp.logical_and(seq + 2 * toward >= 0, seq + 2 * toward < n_seq)
+    is_handed = jnp.logical_and(seq - 2 * toward >= 0, seq - 2 * toward < n_seq)
+
+    def stale_rows(slot):
+        return kv.at[:, pl.ds(slot * TPD + TPP, TPD - TPP)]
+
+    def stale_copy(landing=None):
+        landing = 1 - toward if landing is None else landing
         return pltpu.make_async_remote_copy(
             src_ref=stale_ref.at[:, pl.ds(TPP, TPD - TPP)],
-            dst_ref=kv.at[:, pl.ds((1 - by) * TPD + TPP, TPD - TPP)],
-            send_sem=stale_send.at[1 - by],
-            recv_sem=stale_recv.at[1 - by],
-            device_id=(seg, seq + by),
+            dst_ref=stale_rows(landing),
+            send_sem=stale_send.at[0],
+            recv_sem=stale_recv.at[0],
+            device_id=(seg, seq + toward),
+            device_id_type=MESH,
+        )
+
+    def stale_handed():
+        return pltpu.make_async_remote_copy(
+            src_ref=stale_rows(1 + toward),
+            dst_ref=stale_rows(1 - toward),
+            send_sem=stale_send.at[1],
+            recv_sem=stale_recv.at[1],
+            device_id=(seg, seq + 2 * toward),
             device_id_type=MESH,
         )
 
@@ -194,8 +217,7 @@
     pl.when(odd)(lambda: pl.semaphore_wait(go_sem, 1))
     for part, way in parts:
         ring_copy(0, way, part).start()
-    pl.when(has_left)(lambda: stale_copy(-1).start())
-    pl.when(has_right)(lambda: stale_copy(1).start())
+    stale_copy().start()
 
     def forward(step, carry):
         for part, way in parts:
@@ -205,6 +227,11 @@
         @pl.when(jnp.logical_and(step == n_seq // 2 - 1, jnp.logical_not(odd)))
         def _():
             pl.semaphore_signal(go_sem, inc=1, device_id=(seg + 1, seq), device_id_type=MESH)
+
+        @pl.when(step == n_seq // 2 - 1)
+        def _():
+            stale_copy(1 + toward).wait_recv()
+            pl.when(hands_on)(lambda: stale_handed().start())
 
         return carry
 
@@ -233,8 +260,8 @@
         finish_last()
 
     own_stale.wait()
-    pl.when(has_left)(lambda: stale_copy(1).wait_recv())
-    pl.when(has_right)(lambda: stale_copy(-1).wait_recv())
+    pl.when(is_handed)(lambda: stale_handed().wait_recv())
+    pl.when(hands_on)(lambda: stale_handed().wait_send())
 
     gain_q = gain_q_ref[...]
     gain_k = gain_k_ref[...]
@@ -348,8 +375,7 @@
         return carry
 
     lax.fori_loop(0, n_seq - 1, drain_ring, 0)
-    pl.when(has_left)(lambda: stale_copy(-1).wait_send())
-    pl.when(has_right)(lambda: stale_copy(1).wait_send())
+    stale_copy().wait_send()
 
     def drain_x(patch, carry):
         x_copy(out_ref, patch, 0, seg + 1).wait_send()
@@ -408,8 +434,8 @@
             dma((2, steps)),
             dma((2, steps)),
             pltpu.SemaphoreType.REGULAR,
-            dma((3,)),
-            dma((3,)),
+            dma((2,)),
+            dma((2,)),
             dma((PATCHES, 3)),
             dma((PATCHES, 3)),
         ],

time: 403 us -> 367 us (0.911)
  Pallas kernels: 395 us -> 359 us
    pallas_call x1, Pallas kernels: 395 us -> 359 us  [per_device(): pl.pallas_call(functools.partial(kernel, n_seg, n_seq), out_shape=jax.Sha...]
where the time goes in v4:
time: 367 us; the launch traced here: 364 us
  Pallas kernels  359 us (98%)
    pallas_call x1, Pallas kernels, per_device(): pl.pallas_call(functools.partial(kernel, n_seg, n_seq), out_shape=jax.Sha...  359 us

profile of v4, /device:TPU:19, one launch (start us, length us, event | category | flops | bytes accessed | tf_op | source)
XLA Modules:
  0.0 364.2 jit_solution(3391714060897016664)
XLA Ops:
  0.0 1.3 subtract_select_fusion.tidx_ref
  1.4 0.7 fusion
  2.0 0.1 broadcast_in_dim.14
  2.1 0.7 convert_element_type.15.listed_ref
  2.8 359.0 %shard_map.91 = bf16[3,128,1536]{2,1,0:T(8,128)(2,1)} custom-call(s32[6,6]{1,0:T(8,128)} %subtract_select_fusion.tidx_ref, f32[6,1,384]{2,1,0:T(1,128)} %convert_element_type.15.listed_ref, f32[1,128]{1,0:T(1,128)} %gain_q_ref.1, f32[1,128]{1,0:T(1,128)} %gain_k_ref.1, bf16[3,128,1536]{2,1,0:T(8,128)(2,1)} %bitcast.9, bf16[2,6,64,1536]{3,2,1,0:T(8,128)(2,1)} %bitcast.8, ...), custom_call_target="tpu_custom_call" | custom-call | tf_op jit(solution)/shard_map/pallas_call | solution.py:417
  361.8 2.4 copy.11
  (1 shorter events, 0.0 us)

commit v5 on v4

--- a/solution.py
+++ b/solution.py
@@ -205,9 +205,23 @@
     for load in loads:
         load.wait()
 
+    def latent_handed(patch):
+        return pltpu.make_async_remote_copy(
+            src_ref=xbuf.at[patch, 1 + toward],
+            dst_ref=xbuf.at[patch, 1 - toward],
+            send_sem=x_send.at[patch, 1 + toward],
+            recv_sem=x_recv.at[patch, 1 - toward],
+            device_id=(seg, seq + 2 * toward),
+            device_id_type=MESH,
+        )
+
     def send_latent(patch, carry):
-        pl.when(has_left)(lambda: x_copy(latent_ref, patch, -1, seg).start())
-        pl.when(has_right)(lambda: x_copy(latent_ref, patch, 1, seg).start())
+        x_copy(latent_ref, patch, toward, seg).start()
+        return carry
+
+    def hand_latent(patch, carry):
+        x_copy(latent_ref, patch, -toward, seg).wait_recv()
+        pl.when(hands_on)(lambda: latent_handed(patch).start())
         return carry
 
     @pl.when(seg == 0)
@@ -232,6 +246,10 @@
         def _():
             stale_copy(1 + toward).wait_recv()
             pl.when(hands_on)(lambda: stale_handed().start())
+
+            @pl.when(seg == 0)
+            def _():
+                lax.fori_loop(0, PATCHES, hand_latent, 0)
 
         return carry
 
@@ -266,9 +284,12 @@
     gain_q = gain_q_ref[...]
     gain_k = gain_k_ref[...]
 
+    waits_left = jnp.logical_and(has_left, jnp.logical_or(has_prev, toward == 1))
+    waits_right = jnp.logical_and(has_right, jnp.logical_or(has_prev, toward == -1))
+
     def do_patch(patch, carry):
-        pl.when(has_left)(lambda: x_copy(out_ref, patch, 1, seg).wait_recv())
-        pl.when(has_right)(lambda: x_copy(out_ref, patch, -1, seg).wait_recv())
+        pl.when(waits_left)(lambda: x_copy(out_ref, patch, 1, seg).wait_recv())
+        pl.when(waits_right)(lambda: x_copy(out_ref, patch, -1, seg).wait_recv())
         pl.when(has_prev)(lambda: x_copy(out_ref, patch, 0, seg).wait_recv())
 
         beside_last = jnp.logical_and(early, patch == 0)
@@ -357,8 +378,8 @@
         return carry
 
     def latent_left(patch, carry):
-        pl.when(has_left)(lambda: x_copy(latent_ref, patch, -1, seg).wait_send())
-        pl.when(has_right)(lambda: x_copy(latent_ref, patch, 1, seg).wait_send())
+        x_copy(latent_ref, patch, toward, seg).wait_send()
+        pl.when(hands_on)(lambda: latent_handed(patch).wait_send())
         return carry
 
     @pl.when(seg == 0)

time: 367 us -> 381 us (1.038)
  Pallas kernels: 359 us -> 375 us
    pallas_call x1, Pallas kernels: 359 us -> 375 us  [per_device(): pl.pallas_call(functools.partial(kernel, n_seg, n_seq), out_shape=jax.Sha...]
where the time goes in v5:
time: 381 us; the launch traced here: 380 us
  Pallas kernels  375 us (98%)
    pallas_call x1, Pallas kernels, per_device(): pl.pallas_call(functools.partial(kernel, n_seg, n_seq), out_shape=jax.Sha...  375 us

profile of v5, /device:TPU:19, one launch (start us, length us, event | category | flops | bytes accessed | tf_op | source)
XLA Modules:
  0.0 380.4 jit_solution(5154352029399153280)
XLA Ops:
  0.0 1.3 subtract_select_fusion.tidx_ref
  1.4 0.7 fusion
  2.0 0.1 broadcast_in_dim.14
  2.1 0.7 convert_element_type.15.listed_ref
  2.8 375.2 %shard_map.91 = bf16[3,128,1536]{2,1,0:T(8,128)(2,1)} custom-call(s32[6,6]{1,0:T(8,128)} %subtract_select_fusion.tidx_ref, f32[6,1,384]{2,1,0:T(1,128)} %convert_element_type.15.listed_ref, f32[1,128]{1,0:T(1,128)} %gain_q_ref.1, f32[1,128]{1,0:T(1,128)} %gain_k_ref.1, bf16[3,128,1536]{2,1,0:T(8,128)(2,1)} %bitcast.9, bf16[2,6,64,1536]{3,2,1,0:T(8,128)(2,1)} %bitcast.8, ...), custom_call_target="tpu_custom_call" | custom-call | tf_op jit(solution)/shard_map/pallas_call | solution.py:438
  378.0 2.4 copy.11
  (1 shorter events, 0.0 us)

commit v6 on v4

--- a/solution.py
+++ b/solution.py
@@ -224,7 +224,7 @@
             ring_copy(step - 1, way, part, 1).wait_recv()
             ring_copy(step, way, part).start()
 
-        @pl.when(jnp.logical_and(step == n_seq // 2 - 1, jnp.logical_not(odd)))
+        @pl.when(jnp.logical_and(step == 1, jnp.logical_not(odd)))
         def _():
             pl.semaphore_signal(go_sem, inc=1, device_id=(seg + 1, seq), device_id_type=MESH)
 

time: 367 us -> 391 us (1.065)
  Pallas kernels: 359 us -> 382 us
    pallas_call x1, Pallas kernels: 359 us -> 382 us  [per_device(): pl.pallas_call(functools.partial(kernel, n_seg, n_seq), out_shape=jax.Sha...]
where the time goes in v6:
time: 391 us; the launch traced here: 387 us
  Pallas kernels  382 us (98%)
    pallas_call x1, Pallas kernels, per_device(): pl.pallas_call(functools.partial(kernel, n_seg, n_seq), out_shape=jax.Sha...  382 us

profile of v6, /device:TPU:19, one launch (start us, length us, event | category | flops | bytes accessed | tf_op | source)
XLA Modules:
  0.0 387.3 jit_solution(18042340279885021459)
XLA Ops:
  0.0 1.3 subtract_select_fusion.tidx_ref
  1.4 0.7 fusion
  2.0 0.1 broadcast_in_dim.14
  2.1 0.7 convert_element_type.15.listed_ref
  2.8 382.2 %shard_map.91 = bf16[3,128,1536]{2,1,0:T(8,128)(2,1)} custom-call(s32[6,6]{1,0:T(8,128)} %subtract_select_fusion.tidx_ref, f32[6,1,384]{2,1,0:T(1,128)} %convert_element_type.15.listed_ref, f32[1,128]{1,0:T(1,128)} %gain_q_ref.1, f32[1,128]{1,0:T(1,128)} %gain_k_ref.1, bf16[3,128,1536]{2,1,0:T(8,128)(2,1)} %bitcast.9, bf16[2,6,64,1536]{3,2,1,0:T(8,128)(2,1)} %bitcast.8, ...), custom_call_target="tpu_custom_call" | custom-call | tf_op jit(solution)/shard_map/pallas_call | solution.py:417
  385.0 2.4 copy.11
  (1 shorter events, 0.0 us)
